TPU v7x, 32 devices: a whole 2x2x4 slice. The times are simulated.
32 devices in a mesh: loc: 16 (over z, y, x), sensor: 2 (over core).
Axes of the slice: x: 2, y: 2, z: 4, core: 2. Of those that a mesh axis runs over, the one named last changes fastest.
Arguments:
- tokens: bfloat16 [2, 2048, 2048], P('sensor', 'loc'), may hold values from -6 to 6
- join_weight: bfloat16 [1, 2, 2048, 2048], P(None, 'sensor'), may hold values from -0.125 to 0.125
- join_gain: bfloat16 [1, 2, 2048], P(None, 'sensor'), may hold values from 0.099609375 to 1.8984375
- moe_gain: bfloat16 [1, 2, 2048], P(None, 'sensor'), may hold values from 0.099609375 to 1.8984375
- w_gate: bfloat16 [1, 32, 2048, 1024], P(None, ('loc', 'sensor')), may hold values from -0.125 to 0.125
- w_up: bfloat16 [1, 32, 2048, 1024], P(None, ('loc', 'sensor')), may hold values from -0.125 to 0.125
- w_down: bfloat16 [1, 32, 1024, 2048], P(None, ('loc', 'sensor')), may hold values from -0.1875 to 0.1875
- expert_ids: int32 [1, 2, 2048, 2], P(None, 'sensor', 'loc'), may hold values from 0 to 31, all different within a row; in each aligned block of 128 rows (0 to 127, 128 to 255, ..., all dimensions but the last counted through in order) at most 12 rows name the same one
- gate_scores: float32 [1, 2, 2048, 2], P(None, 'sensor', 'loc'), may hold values from 0.2 to 1
Outputs:
- layer_output: bfloat16 [2, 2048, 2048], P('sensor', 'loc')
Inputs may be any that keep to these rules, and one draw needn't show every extreme that they name: `expert_ids`: take the rows of one layer and sensor in aligned blocks of 128 tokens (the tokens of one index of loc): no expert is named by more than 12 tokens of a block, a bound that some block reaches.
All inputs are finite; a program needn't handle non-finite values.
Results may differ from a plain program's by a relative error of at most 0.012.
Values may be sent and summed in bfloat16 or wider, within the bound.
A program may use at most 128 MiB of HBM per device.

v0:
```python
import jax
import jax.numpy as jnp
from jax import lax
from jax.sharding import PartitionSpec as P


def partner(value, axis, bit):
    return lax.ppermute(value, axis, [(i, i ^ 1 << bit) for i in range(lax.axis_size(axis))])


def norm_rows(values, gain):
    scale = lax.rsqrt(jnp.mean(values * values, axis=-1, keepdims=True) + 1e-05)
    return values * scale * gain.astype(jnp.float32)


def expert_block(received, gate_w, up_w, down_w):
    local_count = gate_w.shape[0]
    grouped = received.reshape((-1, local_count) + received.shape[1:])
    gate_part = jnp.einsum("sjcd,jdf->sjcf", grouped, gate_w, preferred_element_type=jnp.float32)
    up_part = jnp.einsum("sjcd,jdf->sjcf", grouped, up_w, preferred_element_type=jnp.float32)
    hidden = (jax.nn.silu(gate_part) * up_part).astype(jnp.bfloat16)
    result = jnp.einsum(
        "sjcf,jfd->sjcd", hidden, down_w, preferred_element_type=jnp.float32
    ).astype(jnp.bfloat16)
    return result.reshape(received.shape)


def body(tokens, join_weight, join_gain, moe_gain, w_gate, w_up, w_down, expert_ids, gate_scores):
    loc_count = lax.axis_size("loc")
    sensor_count = lax.axis_size("sensor")
    stream = tokens[0]
    tok_rows = stream.shape[0]
    feature_width = stream.shape[1]
    top_count = expert_ids.shape[3]
    local_experts = w_gate.shape[1]
    expert_total = loc_count * sensor_count * local_experts
    capacity = max(2, (3 * top_count * tok_rows + 2 * expert_total - 1) // (2 * expert_total))
    own_gain = join_gain[0, 0]
    other_rows, other_gain = partner((stream, own_gain), "sensor", 0)
    normed = norm_rows(other_rows.astype(jnp.float32), other_gain).astype(jnp.bfloat16)
    projected = jnp.dot(normed, join_weight[0, 0], preferred_element_type=jnp.float32)
    joined_rows = (stream.astype(jnp.float32) + projected).astype(jnp.bfloat16)
    mixed_in = norm_rows(joined_rows.astype(jnp.float32), moe_gain[0, 0]).astype(jnp.bfloat16)
    flat_ids = expert_ids[0, 0].reshape(-1)
    one_hot = (flat_ids[:, None] == jnp.arange(expert_total, dtype=jnp.int32)[None, :]).astype(
        jnp.int32
    )
    earlier = jnp.cumsum(one_hot, axis=0) - one_hot
    slot_index = jnp.sum(earlier * one_hot, axis=1)
    position = flat_ids * capacity + slot_index
    send_rows = jnp.zeros((expert_total * capacity, feature_width), jnp.bfloat16)
    send_rows = send_rows.at[position].set(jnp.repeat(mixed_in, top_count, axis=0))
    send_rows = send_rows.reshape(expert_total, capacity, feature_width)
    gate_w = w_gate[0]
    up_w = w_up[0]
    down_w = w_down[0]
    answered = expert_block(
        lax.all_to_all(send_rows, ("loc", "sensor"), split_axis=0, concat_axis=0, tiled=True),
        gate_w,
        up_w,
        down_w,
    )
    returned = lax.all_to_all(answered, ("loc", "sensor"), split_axis=0, concat_axis=0, tiled=True)
    picked = returned.reshape(expert_total * capacity, feature_width)[position]
    picked = picked.reshape(tok_rows, top_count, feature_width)
    weights_now = gate_scores[0, 0]
    combined = jnp.sum(weights_now[:, :, None] * picked.astype(jnp.float32), axis=1)
    stream = (joined_rows.astype(jnp.float32) + combined).astype(jnp.bfloat16)
    return stream[None]


def solution(mesh):
    placed = (
        P("sensor", "loc", None),
        P(None, "sensor", None, None),
        P(None, "sensor", None),
        P(None, "sensor", None),
        P(None, ("loc", "sensor"), None, None),
        P(None, ("loc", "sensor"), None, None),
        P(None, ("loc", "sensor"), None, None),
        P(None, "sensor", "loc", None),
        P(None, "sensor", "loc", None),
    )
    return jax.shard_map(
        body, mesh=mesh, in_specs=placed, out_specs=P("sensor", "loc", None), check_vma=False
    )
```

profile of v0, /device:TPU:0, one launch (start us, length us, event | category | flops | bytes accessed | tf_op | source)
XLA Modules:
  0.0 153.1 jit_solution(16723150612655698495)
XLA Ops:
  0.0 0.5 collective-permute-start
  0.5 0.7 reduce
  1.2 0.1 collective-permute-start.1
  1.3 0.8 copy.20
  2.1 0.1 eq.29
  2.2 0.1 eq.25
  2.4 0.6 reduce-window.6
  3.0 0.2 slice_reduce_fusion
  3.2 0.7 broadcast_multiply_fusion
  3.9 0.1 copy.19
  4.0 0.1 mul.83
  4.3 0.7 convert_element_type.73
  5.0 0.2 fusion.31
  5.2 4.9 %multiply_reduce_fusion.1 = (f32[128]{0:T(128)S(1)}, f32[128,2048]{1,0:T(8,128)S(1)}) fusion(bf16[1,1,2048,2048]{3,2,1,0:T(8,128)(2,1)} %param.10, bf16[128,2048]{1,0:T(8,128)(2,1)S(1)} %collective-permute-done, f32[2048]{0:T(1024)S(1)} %convert_element_type.59, f32[128]{0:T(128)S(1)} %add_rsqrt_fusion.1, bf16[1,128,2048]{2,1,0:T(8,128)(2,1)} %param.9), kind=kOutput, calls=%fused_computation.32 | convolution fusion | flops 1076363136 | bytes 10494976 | tf_op jit(solution)/shard_map/dot_general | solution.py:41
  10.1 0.2 multiply_convert_fusion
  10.2 0.6 broadcast_in_dim.7
  10.9 0.4 reshape.129
  11.3 3.4 %scatter_custom_fusion = bf16[384,2048]{1,0:T(8,128)(2,1)} fusion(s32[256]{0:T(256)S(1)} %bitcast.106, bf16[256,2048]{1,0:T(8,128)(2,1)S(1)} %reshape.129, bf16[]{:T(256)} %constant.7.clone.1), kind=kCustom, calls=%fused_computation.34 | custom fusion | bytes 1572866 | tf_op jit(solution)/shard_map/scatter | solution.py:52
  14.8 2.4 %reshape.109 = bf16[32,12,2048]{2,1,0:T(8,128)(2,1)S(1)} reshape(bf16[384,2048]{1,0:T(8,128)(2,1)} %scatter_custom_fusion) | data formatting | bytes 3145728 | tf_op jit(solution)/shard_map/reshape | solution.py:53
  17.2 55.8 %all_to_all.10 = bf16[32,12,2048]{2,1,0:T(8,128)(2,1)S(1)} all-to-all(bf16[32,12,2048]{2,1,0:T(8,128)(2,1)S(1)} %reshape.109), channel_id=1, replica_groups=mesh['loc'=16,'sensor'=2] {'loc','sensor'}, dimensions={0} | all-to-all | bytes 3145728 | tf_op jit(solution)/shard_map/all_to_all | solution.py:58
  73.0 1.3 copy-done
  74.3 3.7 %fusion.6 = f32[32,12,1024]{2,0,1:T(8,128)} fusion(bf16[1,1,2048,1024]{3,2,1,0:T(8,128)(2,1)S(1)} %copy-done.2, bf16[32,12,2048]{2,1,0:T(8,128)(2,1)S(1)} %all_to_all.10), kind=kOutput, calls=%fused_computation.8 | convolution fusion | flops 1610612736 | bytes 7340032 | tf_op jit(solution)/shard_map/sjcd,jdf->sjcf/dot_general | solution.py:19
  78.0 8.8 %fusion.8 = bf16[32,12,2048]{2,0,1:T(8,128)(2,1)S(1)} fusion(bf16[1,1,1024,2048]{3,2,1,0:T(8,128)(2,1)} %param.15, bf16[1,1,2048,1024]{3,2,1,0:T(8,128)(2,1)} %param.14, f32[32,12,1024]{2,0,1:T(8,128)} %fusion.6, bf16[32,12,2048]{2,1,0:T(8,128)(2,1)} %copy-done), kind=kOutput, calls=%fused_computation.10 | convolution fusion | flops 3224371200 | bytes 13107200 | tf_op jit(solution)/shard_map/sjcf,jfd->sjcd/dot_general | solution.py:22
  86.9 2.2 %copy.25 = bf16[32,12,2048]{2,1,0:T(8,128)(2,1)} copy(bf16[32,12,2048]{2,0,1:T(8,128)(2,1)S(1)} %fusion.8) | data formatting | bytes 3145728 | tf_op jit(solution)/shard_map/convert_element_type | solution.py:24
  89.1 4.0 %all-to-all-start.1 = ((bf16[32,12,2048]{2,1,0:T(8,128)(2,1)}), bf16[32,12,2048]{2,1,0:T(8,128)(2,1)}, u32[]{:S(2)}, u32[]{:S(2)}) async-start(bf16[32,12,2048]{2,1,0:T(8,128)(2,1)} %copy.25), calls=%async_computation.1 | async-start | bytes 4194304 | tf_op jit(solution)/shard_map/all_to_all | solution.py:63
  93.1 0.1 copy.18
  93.2 48.6 %all-to-all-done.1 = bf16[32,12,2048]{2,1,0:T(8,128)(2,1)} async-done(((bf16[32,12,2048]{2,1,0:T(8,128)(2,1)}), bf16[32,12,2048]{2,1,0:T(8,128)(2,1)}, u32[]{:S(2)}, u32[]{:S(2)}) %all-to-all-start.1) | async-done | bytes 1572896 | tf_op jit(solution)/shard_map/all_to_all | solution.py:63
  141.8 2.5 %reshape.114 = bf16[384,2048]{1,0:T(8,128)(2,1)S(1)} reshape(bf16[32,12,2048]{2,1,0:T(8,128)(2,1)} %all-to-all-done.1) | data formatting | bytes 3145728 | tf_op jit(solution)/shard_map/reshape | solution.py:64
  144.3 2.3 %gather_fusion = bf16[256,2048]{1,0:T(8,128)(2,1)} fusion(bf16[384,2048]{1,0:T(8,128)(2,1)S(1)} %reshape.114, s32[1024]{0:T(1024)S(1)} %pad_clamp_fusion), kind=kCustom, calls=%fused_computation | custom fusion | bytes 2098176 | tf_op jit(solution)/shard_map/gather | solution.py:64
  146.6 2.4 %reshape.116 = f32[128,2,2048]{2,1,0:T(2,128)S(1)} reshape(bf16[256,2048]{1,0:T(8,128)(2,1)} %gather_fusion) | data formatting | bytes 3145728 | tf_op jit(solution)/shard_map/convert_element_type | solution.py:67
  149.0 3.2 %multiply_reduce_fusion = f32[128,2048]{1,0:T(8,128)S(1)} fusion(f32[128,2,2048]{2,1,0:T(2,128)S(1)} %reshape.116, f32[128,2]{1,0:T(8,128)S(1)} %copy.18), kind=kLoop, calls=%fused_computation.14 | loop fusion | flops 786432 | bytes 3146752 | tf_op jit(solution)/shard_map/reduce_sum | solution.py:67
  152.2 0.9 fusion.41
  (16 shorter events, 0.2 us)
Async XLA Ops:
  0.0 5.0 %collective-permute-start = (bf16[128,2048]{1,0:T(8,128)(2,1)}, bf16[128,2048]{1,0:T(8,128)(2,1)S(1)}, u32[]{:S(2)}, u32[]{:S(2)}) collective-permute-start(bf16[128,2048]{1,0:T(8,128)(2,1)} %bitcast.104), channel_id=1, source_target_pairs={{0,1},{1,0},{2,3},{3,2},{4,5},{5,4},{6,7},{7,6},{8,9},{9,8},{10,11... | collective-permute-start | bytes 1572872 | tf_op jit(solution)/shard_map/ppermute | solution.py:8
  1.2 3.8 %collective-permute-start.1 = (bf16[2048]{0:T(1024)(128)(2,1)S(1)}, bf16[2048]{0:T(1024)(128)(2,1)S(1)}, u32[]{:S(2)}, u32[]{:S(2)}) collective-permute-start(bf16[2048]{0:T(1024)(128)(2,1)S(1)} %reduce), channel_id=1, source_target_pairs={{0,1},{1,0},{2,3},{3,2},{4,5},{5,4},{6,7},{7,6},{8,9},{9,8},{10,11... | collective-permute-start | bytes 12296 | tf_op jit(solution)/shard_map/ppermute | solution.py:8
  17.1 57.2 %copy-start.2 = (bf16[1,1,2048,1024]{3,2,1,0:T(8,128)(2,1)S(1)}, bf16[1,1,2048,1024]{3,2,1,0:T(8,128)(2,1)}, u32[]{:S(2)}) copy-start(bf16[1,1,2048,1024]{3,2,1,0:T(8,128)(2,1)} %param.13) | copy-start | bytes 12582916
  73.0 1.4 copy-start
  89.0 4.0 %copy-start.1 = (f32[1,1,128,2]{2,3,1,0:T(2,128)S(1)}, f32[1,1,128,2]{2,3,1,0:T(2,128)}, u32[]{:S(2)}) copy-start(f32[1,1,128,2]{2,3,1,0:T(2,128)} %param.17) | copy-start | bytes 3076
  89.1 52.7 %all-to-all-start.1 = ((bf16[32,12,2048]{2,1,0:T(8,128)(2,1)}), bf16[32,12,2048]{2,1,0:T(8,128)(2,1)}, u32[]{:S(2)}, u32[]{:S(2)}) async-start(bf16[32,12,2048]{2,1,0:T(8,128)(2,1)} %copy.25), calls=%async_computation.1 | async-start | bytes 4194304 | tf_op jit(solution)/shard_map/all_to_all | solution.py:63
where the time goes:
time: 154 us; the launch traced here: 153 us
  blocking collectives  55.8 us (36%)
  waiting for transfers between devices  48.6 us (32%)
  local copies, waits for them, and re-layouts  19.2 us (12%)
  matrix products  17.4 us (11%)
  other arithmetic  7.35 us (5%)
  starting transfers between devices  4.56 us (3%)
    all_to_all x1, blocking collectives, body(): lax.all_to_all(send_rows, ('loc', 'sensor'), split_axis=0, concat_axis=0,...  55.8 us
    all_to_all x1, waiting for transfers between devices, body(): lax.all_to_all(answered, ('loc', 'sensor'), split_axis=0, concat_axis=0,...  48.6 us
    dot_general x1, matrix products, expert_block(): jnp.einsum('sjcf,jfd->sjcd', hidden, down_w, preferred_element_type=jnp.f...  8.81 us
    dot_general x1, matrix products, body(): jnp.dot(normed, join_weight[0, 0], preferred_element_type=jnp.float32)  4.86 us
    all_to_all x1, starting transfers between devices, body(): lax.all_to_all(answered, ('loc', 'sensor'), split_axis=0, concat_axis=0,...  3.99 us
    dot_general x1, matrix products, expert_block(): jnp.einsum('sjcd,jdf->sjcf', grouped, gate_w, preferred_element_type=jnp....  3.73 us
    scatter x1, local copies, waits for them, and re-layouts, body(): send_rows.at[position].set(jnp.repeat(mixed_in, top_count, axis=0))  3.43 us
    reduce_sum x1, other arithmetic, body(): jnp.sum(weights_now[:, :, None] * picked.astype(jnp.float32), axis=1)  3.16 us
  transfers between devices with their start and end apart: 3, of which 1 were waited for; matrix products, arithmetic and copies ran while one was open for 3% of the time, Pallas kernels for 0%

commit v1 on v0

v1 whole, which is shorter than its diff:
```python
import jax
import jax.numpy as jnp
from jax import lax
from jax.sharding import PartitionSpec as P


def partner(value, axis, bit):
    return lax.ppermute(value, axis, [(i, i ^ 1 << bit) for i in range(lax.axis_size(axis))])


def norm_rows(values, gain):
    scale = lax.rsqrt(jnp.mean(values * values, axis=-1, keepdims=True) + 1e-05)
    return values * scale * gain.astype(jnp.float32)


def expert_block(received, gate_w, up_w, down_w):
    rows = received.reshape(-1, received.shape[-1])
    gate_part = jnp.dot(rows, gate_w, preferred_element_type=jnp.float32)
    up_part = jnp.dot(rows, up_w, preferred_element_type=jnp.float32)
    hidden = (jax.nn.silu(gate_part) * up_part).astype(jnp.bfloat16)
    result = jnp.dot(hidden, down_w, preferred_element_type=jnp.float32).astype(jnp.bfloat16)
    return result.reshape(received.shape)


def body(tokens, join_weight, join_gain, moe_gain, w_gate, w_up, w_down, expert_ids, gate_scores):
    loc_count = lax.axis_size("loc")
    sensor_count = lax.axis_size("sensor")
    stream = tokens[0]
    tok_rows = stream.shape[0]
    feature_width = stream.shape[1]
    top_count = expert_ids.shape[3]
    expert_total = loc_count * sensor_count
    capacity = max(2, (3 * top_count * tok_rows + 2 * expert_total - 1) // (2 * expert_total))
    slots = expert_total * capacity
    own_gain = join_gain[0, 0]
    other_rows, other_gain = partner((stream, own_gain), "sensor", 0)
    normed = norm_rows(other_rows.astype(jnp.float32), other_gain).astype(jnp.bfloat16)
    projected = jnp.dot(normed, join_weight[0, 0], preferred_element_type=jnp.float32)
    joined_rows = (stream.astype(jnp.float32) + projected).astype(jnp.bfloat16)
    mixed_in = norm_rows(joined_rows.astype(jnp.float32), moe_gain[0, 0]).astype(jnp.bfloat16)
    ids = expert_ids[0, 0]
    experts = jnp.arange(expert_total, dtype=jnp.int32)
    one_hot = (ids[:, :, None] == experts[None, None, :]).astype(jnp.float32)
    named = jnp.sum(one_hot, axis=1)
    before = jnp.tril(jnp.ones((tok_rows, tok_rows), jnp.float32), -1)
    earlier = jnp.dot(before, named)
    slot_index = jnp.sum(earlier[:, None, :] * one_hot, axis=2).astype(jnp.int32)
    position = ids * capacity + slot_index
    place = position[:, :, None] == jnp.arange(slots, dtype=jnp.int32)[None, None, :]
    spread = jnp.any(place, axis=1).astype(jnp.bfloat16)
    weights = jnp.sum(jnp.where(place, gate_scores[0, 0][:, :, None], 0.0), axis=1)
    high = weights.astype(jnp.bfloat16)
    low = (weights - high.astype(jnp.float32)).astype(jnp.bfloat16)
    send_rows = lax.dot_general(
        spread, mixed_in, (((0,), (0,)), ((), ())), preferred_element_type=jnp.float32
    ).astype(jnp.bfloat16)
    send_rows = send_rows.reshape(expert_total, capacity, feature_width)
    answered = expert_block(
        lax.all_to_all(send_rows, ("loc", "sensor"), split_axis=0, concat_axis=0, tiled=True),
        w_gate[0, 0],
        w_up[0, 0],
        w_down[0, 0],
    )
    returned = lax.all_to_all(answered, ("loc", "sensor"), split_axis=0, concat_axis=0, tiled=True)
    returned = returned.reshape(slots, feature_width)
    combined = jnp.dot(
        jnp.concatenate([high, low], axis=1),
        jnp.concatenate([returned, returned], axis=0),
        preferred_element_type=jnp.float32,
    )
    stream = (joined_rows.astype(jnp.float32) + combined).astype(jnp.bfloat16)
    return stream[None]


def solution(mesh):
    placed = (
        P("sensor", "loc", None),
        P(None, "sensor", None, None),
        P(None, "sensor", None),
        P(None, "sensor", None),
        P(None, ("loc", "sensor"), None, None),
        P(None, ("loc", "sensor"), None, None),
        P(None, ("loc", "sensor"), None, None),
        P(None, "sensor", "loc", None),
        P(None, "sensor", "loc", None),
    )
    return jax.shard_map(
        body, mesh=mesh, in_specs=placed, out_specs=P("sensor", "loc", None), check_vma=False
    )
```

time: 154 us -> 147 us (0.955)
  local copies, waits for them, and re-layouts: 19.2 us -> 9.8 us
  matrix products: 17.4 us -> 23.8 us
  other arithmetic: 7.35 us -> 4 us
    dot_general x2 -> x5, matrix products: 12.5 us -> 19 us  [the longest x1 8.56 us: expert_block(): jnp.dot(hidden, down_w, preferred_element_type=jnp.float32)]
    convert_element_type x2 -> x0, local copies, waits for them, and re-layouts: 4.56 us -> none  [the longest x1 2.37 us: body(): picked.astype(jnp.float32)]
    reshape x2 -> x3, local copies, waits for them, and re-layouts: 2.93 us -> 7.43 us  [the longest x1 3.6 us: expert_block(): return result.reshape(received.shape)]
    scatter x1 -> x0, local copies, waits for them, and re-layouts: 3.43 us -> none  [body(): send_rows.at[position].set(jnp.repeat(mixed_in, top_count, axis=0))]
    gather x1 -> x0, local copies, waits for them, and re-layouts: 2.35 us -> none  [body(): picked = returned.reshape(expert_total * capacity, feature_width)[position]]
    unnamed x7 -> x2, local copies, waits for them, and re-layouts: 2.15 us -> 0.01 us
    reduce_sum x2 -> x3, other arithmetic: 3.26 us -> 1.54 us  [the longest x1 0.72 us: body(): jnp.sum(earlier[:, None, :] * one_hot, axis=2).astype(jnp.int32)]
where the time goes in v1:
time: 147 us
  blocking collectives  55.9 us (38%)
  waiting for transfers between devices  48.7 us (33%)
  matrix products  23.8 us (16%)
  local copies, waits for them, and re-layouts  9.8 us (7%)
  starting transfers between devices  4.24 us (3%)
  other arithmetic  4 us (3%)
    all_to_all x1, blocking collectives, body(): lax.all_to_all(send_rows, ('loc', 'sensor'), split_axis=0, concat_axis=0,...  55.9 us
    all_to_all x1, waiting for transfers between devices, body(): lax.all_to_all(answered, ('loc', 'sensor'), split_axis=0, concat_axis=0,...  48.7 us
    dot_general x1, matrix products, expert_block(): jnp.dot(hidden, down_w, preferred_element_type=jnp.float32)  8.56 us
    dot_general x1, matrix products, expert_block(): gate_part = jnp.dot(rows, gate_w, preferred_element_type=jnp.float32)  5.13 us
    dot_general x1, matrix products, body(): jnp.dot(normed, join_weight[0, 0], preferred_element_type=jnp.float32)  4.86 us
    all_to_all x1, starting transfers between devices, body(): lax.all_to_all(answered, ('loc', 'sensor'), split_axis=0, concat_axis=0,...  3.67 us
    reshape x1, local copies, waits for them, and re-layouts, expert_block(): return result.reshape(received.shape)  3.6 us
    dot_general x1, matrix products, body(): jnp.dot(jnp.concatenate([high, low], axis=1), jnp.concatenate([returned,...  3.28 us
  transfers between devices with their start and end apart: 3, of which 1 were waited for; matrix products, arithmetic and copies ran while one was open for 3% of the time, Pallas kernels for 0%

profile of v1, /device:TPU:0, one launch (start us, length us, event | category | flops | bytes accessed | tf_op | source)
XLA Modules:
  0.0 146.6 jit_solution(4604981035551574675)
XLA Ops:
  0.0 0.5 collective-permute-start
  0.5 0.7 reduce
  1.2 0.1 collective-permute-start.1
  1.3 0.7 convert_reduce_fusion
  2.0 0.2 fusion.50
  2.2 0.7 select_reduce_fusion.1
  2.9 0.7 convert_add_fusion
  3.6 0.1 fusion.46
  3.7 0.7 convert_element_type.82
  4.4 0.0 collective-permute-done.1
  4.4 0.0 collective-permute-done
  4.5 0.2 fusion.35
  4.7 4.9 %multiply_reduce_fusion = (f32[128]{0:T(128)S(1)}, f32[128,2048]{1,0:T(8,128)S(1)}) fusion(bf16[1,1,2048,2048]{3,2,1,0:T(8,128)(2,1)} %param.10, bf16[128,2048]{1,0:T(8,128)(2,1)S(1)} %collective-permute-done, f32[2048]{0:T(1024)S(1)} %convert_element_type.66, f32[128]{0:T(128)S(1)} %add_rsqrt_fusion.1, bf16[1,128,2048]{2,1,0:T(8,128)(2,1)} %param.9), kind=kOutput, calls=%fused_computation.27 | convolution fusion | flops 1076363136 | bytes 10494976 | tf_op jit(solution)/shard_map/dot_general | solution.py:38
  9.5 1.8 %convolution_convert_fusion = bf16[384,2048]{1,0:T(8,128)(2,1)} fusion(pred[128,384]{1,0:T(8,128)(4,1)S(1)} %fusion.46, f32[128,2048]{1,0:T(8,128)S(1)} %get-tuple-element.8, f32[2048]{0:T(1024)S(1)} %bitcast.39, f32[128]{0:T(128)S(1)} %add_rsqrt_fusion), kind=kOutput, calls=%fused_computation.13 | convolution fusion | flops 202899456 | bytes 2679296 | tf_op jit(solution)/shard_map/dot_general | solution.py:54
  11.3 2.4 %reshape.48 = bf16[32,12,2048]{2,1,0:T(8,128)(2,1)S(1)} reshape(bf16[384,2048]{1,0:T(8,128)(2,1)} %convolution_convert_fusion) | data formatting | bytes 3145728 | tf_op jit(solution)/shard_map/reshape | solution.py:57
  13.7 55.9 %all_to_all.10 = bf16[32,12,2048]{2,1,0:T(8,128)(2,1)} all-to-all(bf16[32,12,2048]{2,1,0:T(8,128)(2,1)S(1)} %reshape.48), channel_id=1, replica_groups=mesh['loc'=16,'sensor'=2] {'loc','sensor'}, dimensions={0} | all-to-all | bytes 3145728 | tf_op jit(solution)/shard_map/all_to_all | solution.py:59
  69.6 2.5 %reshape.49 = bf16[384,2048]{1,0:T(8,128)(2,1)S(1)} reshape(bf16[32,12,2048]{2,1,0:T(8,128)(2,1)} %all_to_all.10) | data formatting | bytes 3145728 | tf_op jit(solution)/shard_map/reshape | solution.py:17
  72.1 5.1 %fusion.6 = f32[384,1024]{1,0:T(8,128)} fusion(bf16[384,2048]{1,0:T(8,128)(2,1)S(1)} %reshape.49, bf16[1,1,2048,1024]{3,2,1,0:T(8,128)(2,1)} %param.13), kind=kOutput, calls=%fused_computation.6 | convolution fusion | flops 1610612736 | bytes 7340032 | tf_op jit(solution)/shard_map/dot_general | solution.py:18
  77.3 8.6 %fusion.12 = bf16[384,2048]{1,0:T(8,128)(2,1)} fusion(bf16[1,1,1024,2048]{3,2,1,0:T(8,128)(2,1)} %param.15, f32[384,1024]{1,0:T(8,128)} %fusion.6, bf16[384,2048]{1,0:T(8,128)(2,1)S(1)} %reshape.49, bf16[1,1,2048,1024]{3,2,1,0:T(8,128)(2,1)} %param.14), kind=kOutput, calls=%fused_computation.12 | convolution fusion | flops 3224371200 | bytes 13107200 | tf_op jit(solution)/shard_map/dot_general | solution.py:21
  85.8 3.6 %reshape.50 = bf16[32,12,2048]{2,1,0:T(8,128)(2,1)} reshape(bf16[384,2048]{1,0:T(8,128)(2,1)} %fusion.12) | data formatting | bytes 3145728 | tf_op jit(solution)/shard_map/reshape | solution.py:22
  89.4 0.0 copy-start
  89.4 3.7 %all-to-all-start.1 = ((bf16[32,12,2048]{2,1,0:T(8,128)(2,1)}), bf16[32,12,2048]{2,1,0:T(8,128)(2,1)S(1)}, u32[]{:S(2)}, u32[]{:S(2)}) async-start(bf16[32,12,2048]{2,1,0:T(8,128)(2,1)} %reshape.50), calls=%async_computation.1 | async-start | bytes 4194304 | tf_op jit(solution)/shard_map/all_to_all | solution.py:64
  93.1 0.0 copy-done
  93.1 0.1 select_reduce_fusion
  93.3 48.7 %all-to-all-done.1 = bf16[32,12,2048]{2,1,0:T(8,128)(2,1)S(1)} async-done(((bf16[32,12,2048]{2,1,0:T(8,128)(2,1)}), bf16[32,12,2048]{2,1,0:T(8,128)(2,1)S(1)}, u32[]{:S(2)}, u32[]{:S(2)}) %all-to-all-start.1) | async-done | bytes 1572896 | tf_op jit(solution)/shard_map/all_to_all | solution.py:64
  142.0 1.3 reshape.51
  143.3 3.3 %fusion.30 = bf16[1,128,2048]{2,1,0:T(8,128)(2,1)} fusion(f32[128,2048]{1,0:T(8,128)S(1)} %get-tuple-element.8, bf16[384,2048]{1,0:T(8,128)(2,1)} %reshape.51, bf16[128,384]{1,0:T(8,128)(2,1)S(1)} %get-tuple-element.5, bf16[128,384]{1,0:T(8,128)(2,1)S(1)} %get-tuple-element.6), kind=kOutput, calls=%fused_computation.19 | convolution fusion | flops 409862144 | bytes 3342336 | tf_op jit(solution)/shard_map/dot_general | solution.py:66
  (5 shorter events, 0.0 us)
Async XLA Ops:
  0.0 4.5 %collective-permute-start = (bf16[128,2048]{1,0:T(8,128)(2,1)}, bf16[128,2048]{1,0:T(8,128)(2,1)S(1)}, u32[]{:S(2)}, u32[]{:S(2)}) collective-permute-start(bf16[128,2048]{1,0:T(8,128)(2,1)} %bitcast.38), channel_id=1, source_target_pairs={{0,1},{1,0},{2,3},{3,2},{4,5},{5,4},{6,7},{7,6},{8,9},{9,8},{10,11... | collective-permute-start | bytes 1572872 | tf_op jit(solution)/shard_map/ppermute | solution.py:8
  1.2 3.2 %collective-permute-start.1 = (bf16[2048]{0:T(1024)(128)(2,1)S(1)}, bf16[2048]{0:T(1024)(128)(2,1)S(1)}, u32[]{:S(2)}, u32[]{:S(2)}) collective-permute-start(bf16[2048]{0:T(1024)(128)(2,1)S(1)} %reduce), channel_id=1, source_target_pairs={{0,1},{1,0},{2,3},{3,2},{4,5},{5,4},{6,7},{7,6},{8,9},{9,8},{10,11... | collective-permute-start | bytes 12296 | tf_op jit(solution)/shard_map/ppermute | solution.py:8
  89.4 3.7 %copy-start = (f32[1,1,128,2]{2,3,1,0:T(2,128)S(1)}, f32[1,1,128,2]{2,3,1,0:T(2,128)}, u32[]{:S(2)}) copy-start(f32[1,1,128,2]{2,3,1,0:T(2,128)} %param.17) | copy-start | bytes 3076
  89.4 52.6 %all-to-all-start.1 = ((bf16[32,12,2048]{2,1,0:T(8,128)(2,1)}), bf16[32,12,2048]{2,1,0:T(8,128)(2,1)S(1)}, u32[]{:S(2)}, u32[]{:S(2)}) async-start(bf16[32,12,2048]{2,1,0:T(8,128)(2,1)} %reshape.50), calls=%async_computation.1 | async-start | bytes 4194304 | tf_op jit(solution)/shard_map/all_to_all | solution.py:64

commit v2 on v1

v2 whole, which is shorter than its diff:
```python
import functools
import math
import jax
import jax.numpy as jnp
from jax import lax
from jax.experimental import pallas as pl
from jax.experimental.pallas import tpu as pltpu
from jax.sharding import PartitionSpec as P

MESH = pl.DeviceIdType.MESH


def partner(value, axis, bit):
    return lax.ppermute(value, axis, [(i, i ^ 1 << bit) for i in range(lax.axis_size(axis))])


def norm_rows(values, gain):
    scale = lax.rsqrt(jnp.mean(values * values, axis=-1, keepdims=True) + 1e-05)
    return values * scale * gain.astype(jnp.float32)


def dot(a, b):
    return jnp.dot(a, b, preferred_element_type=jnp.float32)


def kernel(
    dims,
    mixed_ref,
    joined_ref,
    spread_ref,
    weight_ref,
    pack_ref,
    unpack_ref,
    gate_hbm,
    up_hbm,
    down_hbm,
    out_ref,
    gate_ref,
    up_ref,
    down_ref,
    sent,
    got,
    answer,
    back,
    stack,
    rows,
    hidden,
    acc,
    load_sems,
    sent_sems,
    got_sems,
    answer_sems,
    back_sems,
):
    planes, members, sensors, pieces = dims
    total = planes * members
    piece = stack.shape[1]
    plane_rows = rows.shape[0]
    slab = sent.shape[1]
    width = rows.shape[1]
    hidden_width = hidden.shape[1]
    me = lax.axis_index("loc") * sensors + lax.axis_index("sensor")
    my_plane = me // members
    my_place = me % members
    half = planes // 2
    my_half = my_plane // half

    def device(index):
        return (index // sensors, index % sensors)

    loads = [
        pltpu.make_async_copy(src, dst, load_sems.at[i])
        for i, (src, dst) in enumerate(
            ((gate_hbm, gate_ref), (up_hbm, up_ref), (down_hbm, down_ref))
        )
    ]
    for load in loads:
        load.start()

    barrier = pltpu.get_barrier_semaphore()

    def greet(i, _):
        other = lax.rem(me + i, total)
        pl.semaphore_signal(barrier, inc=1, device_id=device(other), device_id_type=MESH)
        return _

    lax.fori_loop(1, total, greet, 0)

    def far(k):
        return (1 - my_half) * half + (my_plane + k) % half

    def near(k):
        return my_half * half + (my_plane + k) % half

    def plane_out(step):
        return jnp.where(step < half, far(step), near(step))

    def plane_in(step):
        return jnp.where(step < half, near(step), far(step))

    def pack(values, target, plane):
        for c in range(pieces):
            stack[c * plane_rows : (c + 1) * plane_rows, :] = values[:, c * piece : (c + 1) * piece]
        packed = dot(pack_ref[...], stack[...]).astype(jnp.bfloat16)
        target[pl.ds(plane * members, members)] = packed.reshape(members, slab, piece)

    def unpack(source, plane):
        values = source[pl.ds(plane * members, members)].reshape(members * slab, piece)
        return dot(unpack_ref[...], values).astype(jnp.bfloat16)

    def copy(source, target, send_sems, recv_sems, other, landing):
        return pltpu.make_async_remote_copy(
            src_ref=source.at[other],
            dst_ref=target.at[landing],
            send_sem=send_sems.at[other],
            recv_sem=recv_sems.at[landing],
            device_id=device(other),
            device_id_type=MESH,
        )

    def send_plane(source, target, send_sems, recv_sems, plane):
        def one(i, _):
            other = plane * members + lax.rem(my_place + i, members)

            @pl.when(other != me)
            def _send():
                copy(source, target, send_sems, recv_sems, other, me).start()

            @pl.when(other == me)
            def _keep():
                target[me] = source[me]

            return _

        lax.fori_loop(0, members, one, 0)

    def await_plane(source, target, send_sems, recv_sems, plane):
        def one(i, _):
            other = plane * members + lax.rem(my_place + i, members)

            @pl.when(other != me)
            def _wait():
                copy(source, target, send_sems, recv_sems, other, other).wait_recv()

            return _

        lax.fori_loop(0, members, one, 0)

    def dispatch(step, _):
        plane = plane_out(step)
        picked = dot(spread_ref[plane], mixed_ref[...]).astype(jnp.bfloat16)
        pack(picked, sent, plane)

        @pl.when(step == 0)
        def _enter():
            pl.semaphore_wait(barrier, total - 1)

        send_plane(sent, got, sent_sems, got_sems, plane)
        return _

    lax.fori_loop(0, planes, dispatch, 0)

    for load in loads:
        load.wait()

    tile = min(256, hidden_width)
    down_tile = min(512, width)

    def experts(step, _):
        plane = plane_in(step)
        await_plane(sent, got, sent_sems, got_sems, plane)
        stack[...] = unpack(got, plane)
        for c in range(pieces):
            rows[:, c * piece : (c + 1) * piece] = stack[c * plane_rows : (c + 1) * plane_rows, :]

        def hide(j, _):
            part = pl.ds(pl.multiple_of(j * tile, tile), tile)
            gate_part = dot(rows[...], gate_ref[:, part])
            up_part = dot(rows[...], up_ref[:, part])
            value = gate_part / (1.0 + jnp.exp(-gate_part)) * up_part
            hidden[:, part] = value.astype(jnp.bfloat16)
            return _

        lax.fori_loop(0, hidden_width // tile, hide, 0)

        def lower(j, _):
            part = pl.ds(pl.multiple_of(j * down_tile, down_tile), down_tile)
            rows[:, part] = dot(hidden[...], down_ref[:, part]).astype(jnp.bfloat16)
            return _

        lax.fori_loop(0, width // down_tile, lower, 0)
        pack(rows, answer, plane)
        send_plane(answer, back, answer_sems, back_sems, plane)
        return _

    lax.fori_loop(0, planes, experts, 0)

    acc[...] = joined_ref[...].astype(jnp.float32)

    def combine(step, _):
        plane = plane_in(step)
        await_plane(answer, back, answer_sems, back_sems, plane)
        stack[...] = unpack(back, plane)
        for c in range(pieces):
            values = stack[c * plane_rows : (c + 1) * plane_rows, :]
            cols = slice(c * piece, (c + 1) * piece)
            acc[:, cols] += dot(weight_ref[plane, 0], values) + dot(weight_ref[plane, 1], values)
        return _

    lax.fori_loop(0, planes, combine, 0)
    out_ref[...] = acc[...].astype(jnp.bfloat16)

    def finish(i, _):
        other = lax.rem(me + i, total)
        copy(sent, got, sent_sems, got_sems, other, me).wait_send()
        copy(answer, back, answer_sems, back_sems, other, me).wait_send()
        return _

    lax.fori_loop(1, total, finish, 0)


def body(tokens, join_weight, join_gain, moe_gain, w_gate, w_up, w_down, expert_ids, gate_scores):
    loc_count = lax.axis_size("loc")
    sensor_count = lax.axis_size("sensor")
    stream = tokens[0]
    tok_rows = stream.shape[0]
    width = stream.shape[1]
    hidden_width = w_gate.shape[3]
    top_count = expert_ids.shape[3]
    expert_total = loc_count * sensor_count
    capacity = max(2, (3 * top_count * tok_rows + 2 * expert_total - 1) // (2 * expert_total))
    planes = 4
    members = expert_total // planes
    plane_rows = members * capacity
    pieces = 16 // math.gcd(16, capacity)
    piece = width // pieces
    slab = pieces * capacity
    own_gain = join_gain[0, 0]
    other_rows, other_gain = partner((stream, own_gain), "sensor", 0)
    normed = norm_rows(other_rows.astype(jnp.float32), other_gain).astype(jnp.bfloat16)
    projected = jnp.dot(normed, join_weight[0, 0], preferred_element_type=jnp.float32)
    joined_rows = (stream.astype(jnp.float32) + projected).astype(jnp.bfloat16)
    mixed_in = norm_rows(joined_rows.astype(jnp.float32), moe_gain[0, 0]).astype(jnp.bfloat16)
    ids = expert_ids[0, 0]
    scores = gate_scores[0, 0]
    experts = jnp.arange(expert_total, dtype=jnp.int32)
    one_hot = (ids[:, :, None] == experts[None, None, :]).astype(jnp.float32)
    named = jnp.sum(one_hot, axis=1)
    before = jnp.tril(jnp.ones((tok_rows, tok_rows), jnp.float32), -1)
    earlier = jnp.dot(before, named)
    slot_index = jnp.sum(earlier[:, None, :] * one_hot, axis=2).astype(jnp.int32)
    position = ids * capacity + slot_index
    slots = jnp.arange(expert_total * capacity, dtype=jnp.int32).reshape(planes, 1, plane_rows)
    place = [position[:, k][None, :, None] == slots for k in range(top_count)]
    weights = sum(jnp.where(place[k], scores[:, k][None, :, None], 0.0) for k in range(top_count))
    high = weights.astype(jnp.bfloat16)
    low = (weights - high.astype(jnp.float32)).astype(jnp.bfloat16)
    weights = jnp.stack([high, low], axis=1)
    slots = slots.reshape(planes, plane_rows, 1)
    spread = sum(
        (slots == position[:, k][None, None, :]).astype(jnp.bfloat16) for k in range(top_count)
    )
    line = jnp.arange(members * slab, dtype=jnp.int32)
    place_of = (line // capacity) % pieces * plane_rows + line // slab * capacity + line % capacity
    pack = (place_of[:, None] == line[None, :]).astype(jnp.bfloat16)
    unpack = (line[:, None] == place_of[None, :]).astype(jnp.bfloat16)
    vmem = pl.BlockSpec(memory_space=pltpu.VMEM)
    hbm = pl.BlockSpec(memory_space=pl.ANY)
    box = pltpu.VMEM((expert_total, slab, piece), jnp.bfloat16)
    out = pl.pallas_call(
        functools.partial(kernel, (planes, members, sensor_count, pieces)),
        out_shape=jax.ShapeDtypeStruct((tok_rows, width), jnp.bfloat16),
        in_specs=[vmem] * 6 + [hbm] * 3,
        out_specs=vmem,
        scratch_shapes=[
            pltpu.VMEM((width, hidden_width), jnp.bfloat16),
            pltpu.VMEM((width, hidden_width), jnp.bfloat16),
            pltpu.VMEM((hidden_width, width), jnp.bfloat16),
            box,
            box,
            box,
            box,
            pltpu.VMEM((pieces * plane_rows, piece), jnp.bfloat16),
            pltpu.VMEM((plane_rows, width), jnp.bfloat16),
            pltpu.VMEM((plane_rows, hidden_width), jnp.bfloat16),
            pltpu.VMEM((tok_rows, width), jnp.float32),
            pltpu.SemaphoreType.DMA((3,)),
            pltpu.SemaphoreType.DMA((expert_total,)),
            pltpu.SemaphoreType.DMA((expert_total,)),
            pltpu.SemaphoreType.DMA((expert_total,)),
            pltpu.SemaphoreType.DMA((expert_total,)),
        ],
        compiler_params=pltpu.CompilerParams(
            collective_id=0, has_side_effects=True, vmem_limit_bytes=52 * 1024 * 1024
        ),
    )(
        mixed_in,
        joined_rows,
        spread,
        weights,
        pack,
        unpack,
        w_gate[0, 0],
        w_up[0, 0],
        w_down[0, 0],
    )
    return out[None]


def solution(mesh):
    placed = (
        P("sensor", "loc", None),
        P(None, "sensor", None, None),
        P(None, "sensor", None),
        P(None, "sensor", None),
        P(None, ("loc", "sensor"), None, None),
        P(None, ("loc", "sensor"), None, None),
        P(None, ("loc", "sensor"), None, None),
        P(None, "sensor", "loc", None),
        P(None, "sensor", "loc", None),
    )
    return jax.shard_map(
        body, mesh=mesh, in_specs=placed, out_specs=P("sensor", "loc", None), check_vma=False
    )
```

time: 147 us -> 92.4 us (0.63)
  the two profiles are of different devices: /device:TPU:0 before, /device:TPU:17 now
where the time goes in v2:
time: 92.4 us; the launch traced here: 92.1 us
  Pallas kernels  79.5 us (86%)
  matrix products  5.09 us (6%)
  other arithmetic  4.45 us (5%)
  local copies, waits for them, and re-layouts  2.14 us (2%)
    pallas_call x1, Pallas kernels, body(): pl.pallas_call(functools.partial(kernel, (planes, members, sensor_count,...  79.5 us
    dot_general x1, matrix products, body(): jnp.dot(normed, join_weight[0, 0], preferred_element_type=jnp.float32)  4.89 us
  transfers between devices with their start and end apart: 2, of which 0 were waited for; matrix products, arithmetic and copies ran while one was open for 5% of the time, Pallas kernels for 0%

profile of v2, /device:TPU:17, one launch (start us, length us, event | category | flops | bytes accessed | tf_op | source)
XLA Modules:
  0.0 92.1 jit_solution(16812529094849697528)
XLA Ops:
  0.0 0.7 reduce
  0.7 0.7 collective-permute-start.1
  1.5 0.1 collective-permute-start
  1.6 0.8 slice_bitcast_fusion.1
  2.3 0.7 convert_reduce_fusion
  3.0 0.2 fusion.21
  3.2 0.7 select_reduce_fusion
  3.9 0.7 convert_add_fusion
  4.6 0.2 fusion.19
  4.8 0.1 fusion.20.spread_ref
  4.9 0.2 fusion.15
  5.1 0.1 pad_maximum_fusion.weight_ref
  5.2 0.7 convert_element_type.101
  5.9 0.0 collective-permute-done.1
  5.9 0.0 collective-permute-done
  5.9 0.2 fusion.8
  6.1 4.9 %fusion.11 = (f32[128]{0:T(128)S(1)}, bf16[128,2048]{1,0:T(8,128)(2,1)S(1)}) fusion(bf16[1,1,2048,2048]{3,2,1,0:T(8,128)(2,1)} %param.10, bf16[128,2048]{1,0:T(8,128)(2,1)S(1)} %collective-permute-done, f32[2048]{0:T(1024)S(1)} %convert_element_type.85, f32[128]{0:T(128)S(1)} %add_rsqrt_fusion.1, bf16[1,128,2048]{2,1,0:T(8,128)(2,1)} %param.9), kind=kOutput, calls=%fused_computation.11 | convolution fusion | flops 1076363136 | bytes 9970688 | tf_op jit(solution)/shard_map/dot_general | solution.py:241
  11.0 0.0 copy-start
  11.0 0.2 fusion.13.mixed_ref
  11.2 0.6 copy-done
  11.8 79.5 %shard_map.91 = bf16[128,2048]{1,0:T(8,128)(2,1)S(1)} custom-call(bf16[128,2048]{1,0:T(8,128)(2,1)S(1)} %fusion.13.mixed_ref, bf16[128,2048]{1,0:T(8,128)(2,1)} %copy-done, bf16[4,96,128]{2,1,0:T(8,128)(2,1)S(1)} %fusion.20.spread_ref, bf16[4,2,128,96]{3,2,1,0:T(8,128)(2,1)S(1)} %pad_maximum_fusion.weight_ref, ...), custom_call_target="tpu_custom_call" | custom-call | tf_op jit(solution)/shard_map/pallas_call | solution.py:270
  91.3 0.8 copy.13
  (7 shorter events, 0.1 us)
Async XLA Ops:
  0.7 5.2 %collective-permute-start.1 = (bf16[2048]{0:T(1024)(128)(2,1)S(1)}, bf16[2048]{0:T(1024)(128)(2,1)S(1)}, u32[]{:S(2)}, u32[]{:S(2)}) collective-permute-start(bf16[2048]{0:T(1024)(128)(2,1)S(1)} %reduce), channel_id=1, source_target_pairs={{0,1},{1,0},{2,3},{3,2},{4,5},{5,4},{6,7},{7,6},{8,9},{9,8},{10,11... | collective-permute-start | bytes 12296 | tf_op jit(solution)/shard_map/ppermute | solution.py:14
  1.5 4.4 %collective-permute-start = (bf16[128,2048]{1,0:T(8,128)(2,1)}, bf16[128,2048]{1,0:T(8,128)(2,1)S(1)}, u32[]{:S(2)}, u32[]{:S(2)}) collective-permute-start(bf16[128,2048]{1,0:T(8,128)(2,1)} %bitcast.32), channel_id=1, source_target_pairs={{0,1},{1,0},{2,3},{3,2},{4,5},{5,4},{6,7},{7,6},{8,9},{9,8},{10,11... | collective-permute-start | bytes 1572872 | tf_op jit(solution)/shard_map/ppermute | solution.py:14
  11.0 0.8 copy-start

commit v3 on v2

v3 whole, which is shorter than its diff:
```python
import functools
import math
import jax
import jax.numpy as jnp
from jax import lax
from jax.experimental import pallas as pl
from jax.experimental.pallas import tpu as pltpu
from jax.sharding import PartitionSpec as P

MESH = pl.DeviceIdType.MESH


def partner(value, axis, bit):
    return lax.ppermute(value, axis, [(i, i ^ 1 << bit) for i in range(lax.axis_size(axis))])


def norm_rows(values, gain):
    scale = lax.rsqrt(jnp.mean(values * values, axis=-1, keepdims=True) + 1e-05)
    return values * scale * gain.astype(jnp.float32)


def dot(a, b):
    return jnp.dot(a, b, preferred_element_type=jnp.float32)


def kernel(
    dims,
    mixed_ref,
    joined_ref,
    spread_ref,
    weight_ref,
    pack_ref,
    unpack_ref,
    gate_hbm,
    up_hbm,
    down_hbm,
    out_ref,
    gate_ref,
    up_ref,
    down_ref,
    foreign,
    partial,
    partial_in,
    sent,
    got,
    answer,
    back,
    stack,
    rows,
    hidden,
    acc,
    load_sems,
    block_sems,
    foreign_sems,
    partial_sems,
    partial_in_sems,
    sent_sems,
    got_sems,
    answer_sems,
    back_sems,
):
    members, sensors, pieces = dims
    mates = 2 * members
    total = 2 * mates
    chunks, _, chunk = mixed_ref.shape
    piece = stack.shape[1]
    slab = sent.shape[3]
    plane_rows = rows.shape[0] // 2
    hidden_width = hidden.shape[1]
    me = lax.axis_index("loc") * sensors + lax.axis_index("sensor")
    base = me // mates * mates
    mine = me % mates
    my_plane = mine // members
    my_place = mine % members
    partner_device = lax.rem(me + mates, total)

    def device(index):
        return (index // sensors, index % sensors)

    loads = [
        pltpu.make_async_copy(src, dst, load_sems.at[i])
        for i, (src, dst) in enumerate(
            ((gate_hbm, gate_ref), (up_hbm, up_ref), (down_hbm, down_ref))
        )
    ]
    for load in loads:
        load.start()

    barrier = pltpu.get_barrier_semaphore()
    pl.semaphore_signal(barrier, inc=1, device_id=device(partner_device), device_id_type=MESH)

    def greet(i, _):
        other = base + lax.rem(mine + i, mates)
        pl.semaphore_signal(barrier, inc=1, device_id=device(other), device_id_type=MESH)
        return _

    lax.fori_loop(1, mates, greet, 0)
    pl.semaphore_wait(barrier, mates)

    def across(source, target, send_sems, recv_sems, c):
        return pltpu.make_async_remote_copy(
            src_ref=source.at[c],
            dst_ref=target.at[c],
            send_sem=send_sems.at[c],
            recv_sem=recv_sems.at[c],
            device_id=device(partner_device),
            device_id_type=MESH,
        )

    def copy(way, q, c, other, landing):
        source, target, send_sems, recv_sems = way
        return pltpu.make_async_remote_copy(
            src_ref=source.at[q, c, other],
            dst_ref=target.at[q, c, landing],
            send_sem=send_sems.at[q, c, other],
            recv_sem=recv_sems.at[q, c, landing],
            device_id=device(base + other),
            device_id_type=MESH,
        )

    out_way = (sent, got, sent_sems, got_sems)
    home_way = (answer, back, answer_sems, back_sems)

    def send_plane(way, q, c, plane):
        def one(i, _):
            other = plane * members + lax.rem(my_place + i, members)

            @pl.when(other != mine)
            def _send():
                copy(way, q, c, other, mine).start()

            @pl.when(other == mine)
            def _keep():
                way[1][q, c, mine] = way[0][q, c, mine]

            return _

        lax.fori_loop(0, members, one, 0)

    def await_all(way, q, c):
        def one(i, _):
            other = lax.rem(mine + i, mates)
            copy(way, q, c, other, other).wait_recv()
            return _

        lax.fori_loop(1, mates, one, 0)

    def pack(values, way, q, c, plane):
        for i in range(pieces):
            stack[i * plane_rows : (i + 1) * plane_rows, :] = values[:, i * piece : (i + 1) * piece]
        packed = dot(pack_ref[...], stack[...]).astype(jnp.bfloat16)
        way[0][q, c, pl.ds(plane * members, members)] = packed.reshape(members, slab, piece)
        send_plane(way, q, c, plane)

    def unpack(way, q, c, plane):
        values = way[1][q, c, pl.ds(plane * members, members)].reshape(members * slab, piece)
        stack[...] = dot(unpack_ref[...], values).astype(jnp.bfloat16)

    def dispatch(q, source, c):
        def one(step, _):
            plane = lax.rem(my_plane + 1 + step, 2)
            picked = dot(spread_ref[q, plane], source[c]).astype(jnp.bfloat16)
            pack(picked, out_way, q, c, plane)
            return _

        lax.fori_loop(0, 2, one, 0)

    tile = min(256, hidden_width)

    def plane_slice(plane):
        return pl.ds(pl.multiple_of(plane * plane_rows, 16), plane_rows)

    def experts(q):
        for c in range(chunks):
            await_all(out_way, q, c)

            def one(plane, _, c=c):
                unpack(out_way, q, c, plane)
                for i in range(pieces):
                    cols = slice(c * chunk + i * piece, c * chunk + (i + 1) * piece)
                    rows[plane_slice(plane), cols] = stack[i * plane_rows : (i + 1) * plane_rows, :]
                return _

            lax.fori_loop(0, 2, one, 0)

        def hide(j, _):
            part = pl.ds(pl.multiple_of(j * tile, tile), tile)
            gate_part = dot(rows[...], gate_ref[:, part])
            up_part = dot(rows[...], up_ref[:, part])
            value = gate_part / (1.0 + jnp.exp(-gate_part)) * up_part
            hidden[:, part] = value.astype(jnp.bfloat16)
            return _

        lax.fori_loop(0, hidden_width // tile, hide, 0)
        for c in range(chunks):
            cols = slice(c * chunk, (c + 1) * chunk)
            rows[:, cols] = dot(hidden[...], down_ref[:, cols]).astype(jnp.bfloat16)

            def one(step, _, c=c, cols=cols):
                plane = lax.rem(my_plane + 1 + step, 2)
                pack(rows[plane_slice(plane), cols], home_way, q, c, plane)
                return _

            lax.fori_loop(0, 2, one, 0)

    def combine(q, c):
        await_all(home_way, q, c)

        def one(plane, _):
            unpack(home_way, q, c, plane)
            for i in range(pieces):
                values = stack[i * plane_rows : (i + 1) * plane_rows, :]
                cols = slice(i * piece, (i + 1) * piece)
                acc[c, :, cols] += dot(weight_ref[q, plane, 0], values) + dot(
                    weight_ref[q, plane, 1], values
                )
            return _

        lax.fori_loop(0, 2, one, 0)

    for c in range(chunks):
        across(mixed_ref, foreign, block_sems, foreign_sems, c).start()
    for c in range(chunks):
        dispatch(0, mixed_ref, c)
    for c in range(chunks):
        across(mixed_ref, foreign, block_sems, foreign_sems, c).wait_recv()
        dispatch(1, foreign, c)
        if c == max(0, chunks - 2):
            for load in loads:
                load.wait()
            experts(0)
    experts(1)
    for c in range(chunks):
        acc[c] = jnp.zeros_like(acc[c])
        combine(1, c)
        partial[c] = acc[c].astype(jnp.bfloat16)
        across(partial, partial_in, partial_sems, partial_in_sems, c).start()
    for c in range(chunks):
        acc[c] = joined_ref[:, c * chunk : (c + 1) * chunk].astype(jnp.float32)
        combine(0, c)
    for c in range(chunks):
        across(partial, partial_in, partial_sems, partial_in_sems, c).wait_recv()
        out_ref[:, c * chunk : (c + 1) * chunk] = (
            acc[c] + partial_in[c].astype(jnp.float32)
        ).astype(jnp.bfloat16)

    def finish(i, _):
        other = lax.rem(mine + i, mates)
        for q in range(2):
            for c in range(chunks):
                copy(out_way, q, c, other, mine).wait_send()
                copy(home_way, q, c, other, mine).wait_send()
        return _

    lax.fori_loop(1, mates, finish, 0)
    for c in range(chunks):
        across(mixed_ref, foreign, block_sems, foreign_sems, c).wait_send()
        across(partial, partial_in, partial_sems, partial_in_sems, c).wait_send()


def body(tokens, join_weight, join_gain, moe_gain, w_gate, w_up, w_down, expert_ids, gate_scores):
    loc_count = lax.axis_size("loc")
    sensor_count = lax.axis_size("sensor")
    stream = tokens[0]
    tok_rows = stream.shape[0]
    width = stream.shape[1]
    hidden_width = w_gate.shape[3]
    top_count = expert_ids.shape[3]
    expert_total = loc_count * sensor_count
    capacity = max(2, (3 * top_count * tok_rows + 2 * expert_total - 1) // (2 * expert_total))
    planes = 4
    mates = expert_total // 2
    members = expert_total // planes
    plane_rows = members * capacity
    pieces = 16 // math.gcd(16, capacity)
    chunks = max(1, min(2, width // (128 * pieces)))
    chunk = width // chunks
    piece = chunk // pieces
    slab = pieces * capacity
    turn = [(i, (i + loc_count // 2) % loc_count) for i in range(loc_count)]
    ids = expert_ids[0, 0]
    scores = gate_scores[0, 0]
    route = (
        jnp.stack([ids, lax.ppermute(ids, "loc", turn)]),
        jnp.stack([scores, lax.ppermute(scores, "loc", turn)]),
    )
    own_gain = join_gain[0, 0]
    other_rows, other_gain = partner((stream, own_gain), "sensor", 0)
    normed = norm_rows(other_rows.astype(jnp.float32), other_gain).astype(jnp.bfloat16)
    projected = jnp.dot(normed, join_weight[0, 0], preferred_element_type=jnp.float32)
    joined_rows = (stream.astype(jnp.float32) + projected).astype(jnp.bfloat16)
    mixed_in = norm_rows(joined_rows.astype(jnp.float32), moe_gain[0, 0]).astype(jnp.bfloat16)
    mixed_in = mixed_in.reshape(tok_rows, chunks, chunk).transpose(1, 0, 2)
    ids, scores = route
    experts = jnp.arange(expert_total, dtype=jnp.int32)
    one_hot = (ids[:, :, :, None] == experts).astype(jnp.float32)
    named = jnp.sum(one_hot, axis=2)
    before = jnp.tril(jnp.ones((tok_rows, tok_rows), jnp.float32), -1)
    earlier = jnp.einsum("ts,qse->qte", before, named)
    slot_index = jnp.sum(earlier[:, :, None, :] * one_hot, axis=3).astype(jnp.int32)
    position = ids * capacity + slot_index
    first = lax.axis_index("loc") // (loc_count // 2) * (mates * capacity)
    slots = first + jnp.arange(mates * capacity, dtype=jnp.int32).reshape(2, 1, plane_rows)
    weights = sum(
        jnp.where(position[:, None, :, k, None] == slots, scores[:, None, :, k, None], 0.0)
        for k in range(top_count)
    )
    high = weights.astype(jnp.bfloat16)
    low = (weights - high.astype(jnp.float32)).astype(jnp.bfloat16)
    weights = jnp.stack([high, low], axis=2)
    slots = slots.reshape(2, plane_rows, 1)
    spread = sum(
        (slots == position[:, None, None, :, k]).astype(jnp.bfloat16) for k in range(top_count)
    )
    line = jnp.arange(members * slab, dtype=jnp.int32)
    place_of = (line // capacity) % pieces * plane_rows + line // slab * capacity + line % capacity
    pack = (place_of[:, None] == line[None, :]).astype(jnp.bfloat16)
    unpack = (line[:, None] == place_of[None, :]).astype(jnp.bfloat16)
    vmem = pl.BlockSpec(memory_space=pltpu.VMEM)
    hbm = pl.BlockSpec(memory_space=pl.ANY)
    box = pltpu.VMEM((2, chunks, mates, slab, piece), jnp.bfloat16)
    whole = pltpu.VMEM((chunks, tok_rows, chunk), jnp.bfloat16)
    pair = pltpu.SemaphoreType.DMA((chunks,))
    each = pltpu.SemaphoreType.DMA((2, chunks, mates))
    out = pl.pallas_call(
        functools.partial(kernel, (members, sensor_count, pieces)),
        out_shape=jax.ShapeDtypeStruct((tok_rows, width), jnp.bfloat16),
        in_specs=[vmem] * 6 + [hbm] * 3,
        out_specs=vmem,
        scratch_shapes=[
            pltpu.VMEM((width, hidden_width), jnp.bfloat16),
            pltpu.VMEM((width, hidden_width), jnp.bfloat16),
            pltpu.VMEM((hidden_width, width), jnp.bfloat16),
            whole,
            whole,
            whole,
            box,
            box,
            box,
            box,
            pltpu.VMEM((pieces * plane_rows, piece), jnp.bfloat16),
            pltpu.VMEM((2 * plane_rows, width), jnp.bfloat16),
            pltpu.VMEM((2 * plane_rows, hidden_width), jnp.bfloat16),
            pltpu.VMEM((chunks, tok_rows, chunk), jnp.float32),
            pltpu.SemaphoreType.DMA((3,)),
            pair,
            pair,
            pair,
            pair,
            each,
            each,
            each,
            each,
        ],
        compiler_params=pltpu.CompilerParams(
            collective_id=0, has_side_effects=True, vmem_limit_bytes=52 * 1024 * 1024
        ),
    )(
        mixed_in,
        joined_rows,
        spread,
        weights,
        pack,
        unpack,
        w_gate[0, 0],
        w_up[0, 0],
        w_down[0, 0],
    )
    return out[None]


def solution(mesh):
    placed = (
        P("sensor", "loc", None),
        P(None, "sensor", None, None),
        P(None, "sensor", None),
        P(None, "sensor", None),
        P(None, ("loc", "sensor"), None, None),
        P(None, ("loc", "sensor"), None, None),
        P(None, ("loc", "sensor"), None, None),
        P(None, "sensor", "loc", None),
        P(None, "sensor", "loc", None),
    )
    return jax.shard_map(
        body, mesh=mesh, in_specs=placed, out_specs=P("sensor", "loc", None), check_vma=False
    )
```

time: 92.4 us -> 102 us (1.10)
  the two profiles are of different devices: /device:TPU:17 before, /device:TPU:0 now
where the time goes in v3:
time: 102 us
  Pallas kernels  83.8 us (82%)
  matrix products  5.09 us (5%)
  starting transfers between devices  4.64 us (5%)
  other arithmetic  4.58 us (4%)
  waiting for transfers between devices  2.41 us (2%)
  local copies, waits for them, and re-layouts  1.38 us (1%)
    pallas_call x1, Pallas kernels, body(): pl.pallas_call(functools.partial(kernel, (members, sensor_count, pieces))...  83.8 us
    dot_general x1, matrix products, body(): jnp.dot(normed, join_weight[0, 0], preferred_element_type=jnp.float32)  4.89 us
    ppermute x1, starting transfers between devices, body(): lax.ppermute(scores, 'loc', turn)  4.04 us
    ppermute x1, waiting for transfers between devices, body(): lax.ppermute(ids, 'loc', turn)  2.4 us
  transfers between devices with their start and end apart: 4, of which 1 were waited for; matrix products, arithmetic and copies ran while one was open for 4% of the time, Pallas kernels for 0%

profile of v3, /device:TPU:0, one launch (start us, length us, event | category | flops | bytes accessed | tf_op | source)
XLA Modules:
  0.0 102.0 jit_solution(15591364241254583516)
XLA Ops:
  0.0 4.0 %collective-permute-start.3 = (f32[128,2]{0,1:T(2,128)}, f32[128,2]{0,1:T(2,128)S(1)}, u32[]{:S(2)}, u32[]{:S(2)}) collective-permute-start(f32[128,2]{0,1:T(2,128)} %bitcast.58), channel_id=1, source_target_pairs={{0,16},{2,18},{4,20},{6,22},{8,24},{10,26},{12,28},{14,30},{16,0},... | collective-permute-start | bytes 3080 | tf_op jit(solution)/shard_map/ppermute | solution.py:285
  4.0 0.0 collective-permute-start.2
  4.1 0.7 reduce
  4.8 0.1 collective-permute-start.1
  4.9 0.5 collective-permute-start
  5.4 0.2 fusion.15
  5.6 0.7 convert_element_type.101
  6.3 2.4 %collective-permute-done.2 = s32[128,2]{0,1:T(2,128)S(1)} collective-permute-done((s32[128,2]{0,1:T(2,128)}, s32[128,2]{0,1:T(2,128)S(1)}, u32[]{:S(2)}, u32[]{:S(2)}) %collective-permute-start.2) | collective-permute-done | bytes 1056 | tf_op jit(solution)/shard_map/ppermute | solution.py:284
  8.7 0.7 pad_add_fusion
  9.4 0.2 convolution_bitcast_fusion
  9.7 0.7 convert_add_fusion
  10.4 0.0 collective-permute-done.3
  10.4 0.8 fusion.39
  11.1 0.1 fusion.20.spread_ref
  11.2 0.2 fusion.19
  11.4 0.1 pad_maximum_fusion.weight_ref
  11.5 0.0 collective-permute-done.1
  11.5 0.0 collective-permute-done
  11.5 0.2 fusion.8
  11.7 4.9 %fusion.11 = (f32[128]{0:T(128)S(1)}, bf16[128,2048]{1,0:T(8,128)(2,1)S(1)}) fusion(bf16[1,1,2048,2048]{3,2,1,0:T(8,128)(2,1)} %param.10, bf16[128,2048]{1,0:T(8,128)(2,1)S(1)} %collective-permute-done, f32[2048]{0:T(1024)S(1)} %convert_element_type.85, f32[128]{0:T(128)S(1)} %add_rsqrt_fusion.1, bf16[1,128,2048]{2,1,0:T(8,128)(2,1)} %param.9), kind=kOutput, calls=%fused_computation.12 | convolution fusion | flops 1076363136 | bytes 9970688 | tf_op jit(solution)/shard_map/dot_general | solution.py:290
  16.6 0.0 copy-start
  16.7 0.2 fusion.13
  16.9 0.5 copy-done
  17.4 83.8 %shard_map.91 = bf16[128,2048]{1,0:T(8,128)(2,1)S(1)} custom-call(bf16[2,128,1024]{2,1,0:T(8,128)(2,1)S(1)} %bitcast.39, bf16[128,2048]{1,0:T(8,128)(2,1)} %copy-done, bf16[2,2,96,128]{3,2,1,0:T(8,128)(2,1)S(1)} %fusion.20.spread_ref, bf16[2,2,2,128,96]{4,3,2,1,0:T(8,128)(2,1)S(1)} %pad_maximum_fusion.weight_ref, ...), custom_call_target="tpu_custom_call" | custom-call | tf_op jit(solution)/shard_map/pallas_call | solution.py:325
  101.3 0.8 copy.18
  (10 shorter events, 0.1 us)
Async XLA Ops:
  0.0 10.4 %collective-permute-start.3 = (f32[128,2]{0,1:T(2,128)}, f32[128,2]{0,1:T(2,128)S(1)}, u32[]{:S(2)}, u32[]{:S(2)}) collective-permute-start(f32[128,2]{0,1:T(2,128)} %bitcast.58), channel_id=1, source_target_pairs={{0,16},{2,18},{4,20},{6,22},{8,24},{10,26},{12,28},{14,30},{16,0},... | collective-permute-start | bytes 3080 | tf_op jit(solution)/shard_map/ppermute | solution.py:285
  4.0 4.7 %collective-permute-start.2 = (s32[128,2]{0,1:T(2,128)}, s32[128,2]{0,1:T(2,128)S(1)}, u32[]{:S(2)}, u32[]{:S(2)}) collective-permute-start(s32[128,2]{0,1:T(2,128)} %bitcast.53), channel_id=1, source_target_pairs={{0,16},{2,18},{4,20},{6,22},{8,24},{10,26},{12,28},{14,30},{16,0},... | collective-permute-start | bytes 3080 | tf_op jit(solution)/shard_map/ppermute | solution.py:284
  4.8 6.7 %collective-permute-start.1 = (bf16[2048]{0:T(1024)(128)(2,1)S(1)}, bf16[2048]{0:T(1024)(128)(2,1)S(1)}, u32[]{:S(2)}, u32[]{:S(2)}) collective-permute-start(bf16[2048]{0:T(1024)(128)(2,1)S(1)} %reduce), channel_id=1, source_target_pairs={{0,1},{1,0},{2,3},{3,2},{4,5},{5,4},{6,7},{7,6},{8,9},{9,8},{10,11... | collective-permute-start | bytes 12296 | tf_op jit(solution)/shard_map/ppermute | solution.py:14
  4.9 6.7 %collective-permute-start = (bf16[128,2048]{1,0:T(8,128)(2,1)}, bf16[128,2048]{1,0:T(8,128)(2,1)S(1)}, u32[]{:S(2)}, u32[]{:S(2)}) collective-permute-start(bf16[128,2048]{1,0:T(8,128)(2,1)} %bitcast.45), channel_id=1, source_target_pairs={{0,1},{1,0},{2,3},{3,2},{4,5},{5,4},{6,7},{7,6},{8,9},{9,8},{10,11... | collective-permute-start | bytes 1572872 | tf_op jit(solution)/shard_map/ppermute | solution.py:14
  16.6 0.8 copy-start

commit v4 on v2

--- a/solution.py
+++ b/solution.py
@@ -10,10 +10,6 @@
 MESH = pl.DeviceIdType.MESH
 
 
-def partner(value, axis, bit):
-    return lax.ppermute(value, axis, [(i, i ^ 1 << bit) for i in range(lax.axis_size(axis))])
-
-
 def norm_rows(values, gain):
     scale = lax.rsqrt(jnp.mean(values * values, axis=-1, keepdims=True) + 1e-05)
     return values * scale * gain.astype(jnp.float32)
@@ -25,16 +21,19 @@
 
 def kernel(
     dims,
-    mixed_ref,
-    joined_ref,
-    spread_ref,
-    weight_ref,
+    stream_ref,
+    join_gain_ref,
+    moe_gain_ref,
+    ids_ref,
+    scores_ref,
     pack_ref,
     unpack_ref,
+    join_hbm,
     gate_hbm,
     up_hbm,
     down_hbm,
     out_ref,
+    join_ref,
     gate_ref,
     up_ref,
     down_ref,
@@ -46,13 +45,20 @@
     rows,
     hidden,
     acc,
+    normed,
+    normed_in,
+    joined,
+    mixed,
+    spread,
+    weight,
     load_sems,
+    swap_sems,
     sent_sems,
     got_sems,
     answer_sems,
     back_sems,
 ):
-    planes, members, sensors, pieces = dims
+    planes, members, sensors, pieces, capacity = dims
     total = planes * members
     piece = stack.shape[1]
     plane_rows = rows.shape[0]
@@ -68,14 +74,14 @@
     def device(index):
         return (index // sensors, index % sensors)
 
+    join_load = pltpu.make_async_copy(join_hbm, join_ref, load_sems.at[3])
+    join_load.start()
     loads = [
         pltpu.make_async_copy(src, dst, load_sems.at[i])
         for i, (src, dst) in enumerate(
             ((gate_hbm, gate_ref), (up_hbm, up_ref), (down_hbm, down_ref))
         )
     ]
-    for load in loads:
-        load.start()
 
     barrier = pltpu.get_barrier_semaphore()
 
@@ -86,6 +92,59 @@
 
     lax.fori_loop(1, total, greet, 0)
 
+    normed[...] = norm_rows(stream_ref[...].astype(jnp.float32), join_gain_ref[...]).astype(
+        jnp.bfloat16
+    )
+    pl.semaphore_wait(barrier, total - 1)
+    swap = pltpu.make_async_remote_copy(
+        src_ref=normed,
+        dst_ref=normed_in,
+        send_sem=swap_sems.at[0],
+        recv_sem=swap_sems.at[1],
+        device_id=(lax.axis_index("loc"), 1 - lax.axis_index("sensor")),
+        device_id_type=MESH,
+    )
+    swap.start()
+
+    tok_rows = stream_ref.shape[0]
+    ids = ids_ref[...]
+    scores = scores_ref[...]
+    top_count = ids.shape[1]
+    expert = lax.broadcasted_iota(jnp.int32, (tok_rows, total), 1)
+    chosen = [(ids[:, k : k + 1] == expert).astype(jnp.float32) for k in range(top_count)]
+    lower_rows = lax.broadcasted_iota(jnp.int32, (tok_rows, tok_rows), 0)
+    lower_cols = lax.broadcasted_iota(jnp.int32, (tok_rows, tok_rows), 1)
+    before = (lower_cols < lower_rows).astype(jnp.float32).astype(jnp.bfloat16)
+    earlier = dot(before, sum(chosen).astype(jnp.bfloat16))
+    position = [
+        ids[:, k : k + 1] * capacity
+        + jnp.sum(earlier * chosen[k], axis=1, keepdims=True).astype(jnp.int32)
+        for k in range(top_count)
+    ]
+    for plane in range(planes):
+        slot = plane * plane_rows + lax.broadcasted_iota(jnp.int32, (tok_rows, plane_rows), 1)
+        taken = [position[k] == slot for k in range(top_count)]
+        spread[plane] = sum(jnp.where(t, 1.0, 0.0) for t in taken).astype(jnp.bfloat16)
+        value = sum(jnp.where(taken[k], scores[:, k : k + 1], 0.0) for k in range(top_count))
+        high = value.astype(jnp.bfloat16)
+        weight[plane, 0] = high
+        weight[plane, 1] = (value - high.astype(jnp.float32)).astype(jnp.bfloat16)
+
+    swap.wait()
+    join_load.wait()
+    for load in loads:
+        load.start()
+    join_tile = min(512, width)
+
+    def join(j, _):
+        part = pl.ds(pl.multiple_of(j * join_tile, join_tile), join_tile)
+        value = stream_ref[:, part].astype(jnp.float32) + dot(normed_in[...], join_ref[:, part])
+        joined[:, part] = value.astype(jnp.bfloat16)
+        return _
+
+    lax.fori_loop(0, width // join_tile, join, 0)
+    mixed[...] = norm_rows(joined[...].astype(jnp.float32), moe_gain_ref[...]).astype(jnp.bfloat16)
+
     def far(k):
         return (1 - my_half) * half + (my_plane + k) % half
 
@@ -96,7 +155,7 @@
         return jnp.where(step < half, far(step), near(step))
 
     def plane_in(step):
-        return jnp.where(step < half, near(step), far(step))
+        return jnp.where(step % 2 == 0, near(step // 2), far(step // 2))
 
     def pack(values, target, plane):
         for c in range(pieces):
@@ -148,13 +207,13 @@
 
     def dispatch(step, _):
         plane = plane_out(step)
-        picked = dot(spread_ref[plane], mixed_ref[...]).astype(jnp.bfloat16)
+        picked = lax.dot_general(
+            spread[plane],
+            mixed[...],
+            (((0,), (0,)), ((), ())),
+            preferred_element_type=jnp.float32,
+        ).astype(jnp.bfloat16)
         pack(picked, sent, plane)
-
-        @pl.when(step == 0)
-        def _enter():
-            pl.semaphore_wait(barrier, total - 1)
-
         send_plane(sent, got, sent_sems, got_sems, plane)
         return _
 
@@ -195,7 +254,7 @@
 
     lax.fori_loop(0, planes, experts, 0)
 
-    acc[...] = joined_ref[...].astype(jnp.float32)
+    acc[...] = joined[...].astype(jnp.float32)
 
     def combine(step, _):
         plane = plane_in(step)
@@ -204,7 +263,7 @@
         for c in range(pieces):
             values = stack[c * plane_rows : (c + 1) * plane_rows, :]
             cols = slice(c * piece, (c + 1) * piece)
-            acc[:, cols] += dot(weight_ref[plane, 0], values) + dot(weight_ref[plane, 1], values)
+            acc[:, cols] += dot(weight[plane, 0], values) + dot(weight[plane, 1], values)
         return _
 
     lax.fori_loop(0, planes, combine, 0)
@@ -235,31 +294,6 @@
     pieces = 16 // math.gcd(16, capacity)
     piece = width // pieces
     slab = pieces * capacity
-    own_gain = join_gain[0, 0]
-    other_rows, other_gain = partner((stream, own_gain), "sensor", 0)
-    normed = norm_rows(other_rows.astype(jnp.float32), other_gain).astype(jnp.bfloat16)
-    projected = jnp.dot(normed, join_weight[0, 0], preferred_element_type=jnp.float32)
-    joined_rows = (stream.astype(jnp.float32) + projected).astype(jnp.bfloat16)
-    mixed_in = norm_rows(joined_rows.astype(jnp.float32), moe_gain[0, 0]).astype(jnp.bfloat16)
-    ids = expert_ids[0, 0]
-    scores = gate_scores[0, 0]
-    experts = jnp.arange(expert_total, dtype=jnp.int32)
-    one_hot = (ids[:, :, None] == experts[None, None, :]).astype(jnp.float32)
-    named = jnp.sum(one_hot, axis=1)
-    before = jnp.tril(jnp.ones((tok_rows, tok_rows), jnp.float32), -1)
-    earlier = jnp.dot(before, named)
-    slot_index = jnp.sum(earlier[:, None, :] * one_hot, axis=2).astype(jnp.int32)
-    position = ids * capacity + slot_index
-    slots = jnp.arange(expert_total * capacity, dtype=jnp.int32).reshape(planes, 1, plane_rows)
-    place = [position[:, k][None, :, None] == slots for k in range(top_count)]
-    weights = sum(jnp.where(place[k], scores[:, k][None, :, None], 0.0) for k in range(top_count))
-    high = weights.astype(jnp.bfloat16)
-    low = (weights - high.astype(jnp.float32)).astype(jnp.bfloat16)
-    weights = jnp.stack([high, low], axis=1)
-    slots = slots.reshape(planes, plane_rows, 1)
-    spread = sum(
-        (slots == position[:, k][None, None, :]).astype(jnp.bfloat16) for k in range(top_count)
-    )
     line = jnp.arange(members * slab, dtype=jnp.int32)
     place_of = (line // capacity) % pieces * plane_rows + line // slab * capacity + line % capacity
     pack = (place_of[:, None] == line[None, :]).astype(jnp.bfloat16)
@@ -268,11 +302,12 @@
     hbm = pl.BlockSpec(memory_space=pl.ANY)
     box = pltpu.VMEM((expert_total, slab, piece), jnp.bfloat16)
     out = pl.pallas_call(
-        functools.partial(kernel, (planes, members, sensor_count, pieces)),
+        functools.partial(kernel, (planes, members, sensor_count, pieces, capacity)),
         out_shape=jax.ShapeDtypeStruct((tok_rows, width), jnp.bfloat16),
-        in_specs=[vmem] * 6 + [hbm] * 3,
+        in_specs=[vmem] * 7 + [hbm] * 4,
         out_specs=vmem,
         scratch_shapes=[
+            pltpu.VMEM((width, width), jnp.bfloat16),
             pltpu.VMEM((width, hidden_width), jnp.bfloat16),
             pltpu.VMEM((width, hidden_width), jnp.bfloat16),
             pltpu.VMEM((hidden_width, width), jnp.bfloat16),
@@ -284,7 +319,14 @@
             pltpu.VMEM((plane_rows, width), jnp.bfloat16),
             pltpu.VMEM((plane_rows, hidden_width), jnp.bfloat16),
             pltpu.VMEM((tok_rows, width), jnp.float32),
-            pltpu.SemaphoreType.DMA((3,)),
+            pltpu.VMEM((tok_rows, width), jnp.bfloat16),
+            pltpu.VMEM((tok_rows, width), jnp.bfloat16),
+            pltpu.VMEM((tok_rows, width), jnp.bfloat16),
+            pltpu.VMEM((tok_rows, width), jnp.bfloat16),
+            pltpu.VMEM((planes, tok_rows, plane_rows), jnp.bfloat16),
+            pltpu.VMEM((planes, 2, tok_rows, plane_rows), jnp.bfloat16),
+            pltpu.SemaphoreType.DMA((4,)),
+            pltpu.SemaphoreType.DMA((2,)),
             pltpu.SemaphoreType.DMA((expert_total,)),
             pltpu.SemaphoreType.DMA((expert_total,)),
             pltpu.SemaphoreType.DMA((expert_total,)),
@@ -294,12 +336,14 @@
             collective_id=0, has_side_effects=True, vmem_limit_bytes=52 * 1024 * 1024
         ),
     )(
-        mixed_in,
-        joined_rows,
-        spread,
-        weights,
+        stream,
+        join_gain[0],
+        moe_gain[0],
+        expert_ids[0, 0],
+        gate_scores[0, 0],
         pack,
         unpack,
+        join_weight[0, 0],
         w_gate[0, 0],
         w_up[0, 0],
         w_down[0, 0],

time: 92.4 us -> 85.8 us (0.929)
  the two profiles are of different devices: /device:TPU:17 before, /device:TPU:11 now
where the time goes in v4:
time: 85.8 us; the launch traced here: 85.5 us
  Pallas kernels  80.5 us (94%)
  local copies, waits for them, and re-layouts  4.79 us (6%)
    pallas_call x1, Pallas kernels, body(): pl.pallas_call(functools.partial(kernel, (planes, members, sensor_count,...  80.5 us
    unnamed x9, local copies, waits for them, and re-layouts  4.79 us

profile of v4, /device:TPU:11, one launch (start us, length us, event | category | flops | bytes accessed | tf_op | source)
XLA Modules:
  0.0 85.5 jit_solution(8974902177238535202)
XLA Ops:
  0.0 0.8 copy.10
  0.8 0.8 copy.11
  1.6 0.2 fusion.1
  1.8 0.0 copy-start
  1.8 1.0 %copy-done = bf16[1,128,2048]{2,1,0:T(8,128)(2,1)S(1)} copy-done((bf16[1,128,2048]{2,1,0:T(8,128)(2,1)S(1)}, bf16[1,128,2048]{2,1,0:T(8,128)(2,1)}, u32[]{:S(2)}) %copy-start) | copy-done | bytes 524312
  2.8 0.0 copy-start.1
  2.8 0.7 copy-done.1
  3.5 0.0 copy-start.2
  3.5 0.7 copy-done.2
  4.2 80.5 %shard_map.91 = bf16[128,2048]{1,0:T(8,128)(2,1)S(1)} custom-call(bf16[128,2048]{1,0:T(8,128)(2,1)S(1)} %bitcast.11, bf16[1,2048]{1,0:T(2,128)(2,1)S(1)} %bitcast.14, bf16[1,2048]{1,0:T(2,128)(2,1)S(1)} %bitcast.15, s32[128,2]{1,0:T(8,128)S(1)} %bitcast.12, f32[128,2]{1,0:T(8,128)S(1)} %bitcast.13, bf16[384,384]{1,0:T(8,128)(2,1)S(1)} %get-tuple-element.6.pack_ref, ...), custom_call_target="tpu_custom_call" | custom-call | tf_op jit(solution)/shard_map/pallas_call | solution.py:304
  84.7 0.8 copy.13
  (1 shorter events, 0.0 us)
Async XLA Ops:
  1.8 1.0 %copy-start = (bf16[1,128,2048]{2,1,0:T(8,128)(2,1)S(1)}, bf16[1,128,2048]{2,1,0:T(8,128)(2,1)}, u32[]{:S(2)}) copy-start(bf16[1,128,2048]{2,1,0:T(8,128)(2,1)} %param.9) | copy-start | bytes 1572868
  2.8 0.7 copy-start.1
  3.5 0.7 copy-start.2

commit v5 on v4

--- a/solution.py
+++ b/solution.py
@@ -21,6 +21,16 @@
 
 def kernel(
     dims,
+    stream_hbm,
+    join_gain_hbm,
+    moe_gain_hbm,
+    ids_hbm,
+    scores_hbm,
+    join_hbm,
+    gate_hbm,
+    up_hbm,
+    down_hbm,
+    out_ref,
     stream_ref,
     join_gain_ref,
     moe_gain_ref,
@@ -28,11 +38,6 @@
     scores_ref,
     pack_ref,
     unpack_ref,
-    join_hbm,
-    gate_hbm,
-    up_hbm,
-    down_hbm,
-    out_ref,
     join_ref,
     gate_ref,
     up_ref,
@@ -74,6 +79,20 @@
     def device(index):
         return (index // sensors, index % sensors)
 
+    first_loads = [
+        pltpu.make_async_copy(src, dst, load_sems.at[4 + i])
+        for i, (src, dst) in enumerate(
+            (
+                (stream_hbm, stream_ref),
+                (join_gain_hbm, join_gain_ref),
+                (moe_gain_hbm, moe_gain_ref),
+                (ids_hbm, ids_ref),
+                (scores_hbm, scores_ref),
+            )
+        )
+    ]
+    for load in first_loads:
+        load.start()
     join_load = pltpu.make_async_copy(join_hbm, join_ref, load_sems.at[3])
     join_load.start()
     loads = [
@@ -92,6 +111,8 @@
 
     lax.fori_loop(1, total, greet, 0)
 
+    for load in first_loads:
+        load.wait()
     normed[...] = norm_rows(stream_ref[...].astype(jnp.float32), join_gain_ref[...]).astype(
         jnp.bfloat16
     )
@@ -107,17 +128,25 @@
     swap.start()
 
     tok_rows = stream_ref.shape[0]
-    ids = ids_ref[...]
-    scores = scores_ref[...]
-    top_count = ids.shape[1]
+    top_count = ids_ref.shape[0]
     expert = lax.broadcasted_iota(jnp.int32, (tok_rows, total), 1)
-    chosen = [(ids[:, k : k + 1] == expert).astype(jnp.float32) for k in range(top_count)]
     lower_rows = lax.broadcasted_iota(jnp.int32, (tok_rows, tok_rows), 0)
     lower_cols = lax.broadcasted_iota(jnp.int32, (tok_rows, tok_rows), 1)
+
+    def column(line):
+        square = jnp.where(lower_rows == lower_cols, line, 0.0)
+        return jnp.sum(square, axis=1, keepdims=True)
+
+    ids = [
+        column(ids_ref[k : k + 1, :].astype(jnp.float32)).astype(jnp.int32)
+        for k in range(top_count)
+    ]
+    scores = [column(scores_ref[k : k + 1, :]) for k in range(top_count)]
+    chosen = [(ids[k] == expert).astype(jnp.float32) for k in range(top_count)]
     before = (lower_cols < lower_rows).astype(jnp.float32).astype(jnp.bfloat16)
     earlier = dot(before, sum(chosen).astype(jnp.bfloat16))
     position = [
-        ids[:, k : k + 1] * capacity
+        ids[k] * capacity
         + jnp.sum(earlier * chosen[k], axis=1, keepdims=True).astype(jnp.int32)
         for k in range(top_count)
     ]
@@ -125,10 +154,25 @@
         slot = plane * plane_rows + lax.broadcasted_iota(jnp.int32, (tok_rows, plane_rows), 1)
         taken = [position[k] == slot for k in range(top_count)]
         spread[plane] = sum(jnp.where(t, 1.0, 0.0) for t in taken).astype(jnp.bfloat16)
-        value = sum(jnp.where(taken[k], scores[:, k : k + 1], 0.0) for k in range(top_count))
+        value = sum(jnp.where(taken[k], scores[k], 0.0) for k in range(top_count))
         high = value.astype(jnp.bfloat16)
         weight[plane, 0] = high
         weight[plane, 1] = (value - high.astype(jnp.float32)).astype(jnp.bfloat16)
+
+    line_count = members * slab
+
+    def place_of(axis):
+        line = lax.broadcasted_iota(jnp.int32, (line_count, line_count), axis).astype(jnp.float32)
+        member = jnp.floor((line + 0.5) * (1.0 / slab))
+        inside = line - member * slab
+        which = jnp.floor((inside + 0.5) * (1.0 / capacity))
+        return which * plane_rows + member * capacity + (inside - which * capacity)
+
+    for axis, target in ((0, pack_ref), (1, unpack_ref)):
+        line = lax.broadcasted_iota(jnp.int32, (line_count, line_count), 1 - axis)
+        target[...] = jnp.where(place_of(axis) == line.astype(jnp.float32), 1.0, 0.0).astype(
+            jnp.bfloat16
+        )
 
     swap.wait()
     join_load.wait()
@@ -294,19 +338,22 @@
     pieces = 16 // math.gcd(16, capacity)
     piece = width // pieces
     slab = pieces * capacity
-    line = jnp.arange(members * slab, dtype=jnp.int32)
-    place_of = (line // capacity) % pieces * plane_rows + line // slab * capacity + line % capacity
-    pack = (place_of[:, None] == line[None, :]).astype(jnp.bfloat16)
-    unpack = (line[:, None] == place_of[None, :]).astype(jnp.bfloat16)
     vmem = pl.BlockSpec(memory_space=pltpu.VMEM)
-    hbm = pl.BlockSpec(memory_space=pl.ANY)
+    hbm = pl.BlockSpec(memory_space=pltpu.HBM)
     box = pltpu.VMEM((expert_total, slab, piece), jnp.bfloat16)
     out = pl.pallas_call(
         functools.partial(kernel, (planes, members, sensor_count, pieces, capacity)),
         out_shape=jax.ShapeDtypeStruct((tok_rows, width), jnp.bfloat16),
-        in_specs=[vmem] * 7 + [hbm] * 4,
+        in_specs=[hbm] * 9,
         out_specs=vmem,
         scratch_shapes=[
+            pltpu.VMEM((tok_rows, width), jnp.bfloat16),
+            pltpu.VMEM((1, width), jnp.bfloat16),
+            pltpu.VMEM((1, width), jnp.bfloat16),
+            pltpu.VMEM((top_count, tok_rows), jnp.int32),
+            pltpu.VMEM((top_count, tok_rows), jnp.float32),
+            pltpu.VMEM((members * slab, pieces * plane_rows), jnp.bfloat16),
+            pltpu.VMEM((pieces * plane_rows, members * slab), jnp.bfloat16),
             pltpu.VMEM((width, width), jnp.bfloat16),
             pltpu.VMEM((width, hidden_width), jnp.bfloat16),
             pltpu.VMEM((width, hidden_width), jnp.bfloat16),
@@ -325,7 +372,7 @@
             pltpu.VMEM((tok_rows, width), jnp.bfloat16),
             pltpu.VMEM((planes, tok_rows, plane_rows), jnp.bfloat16),
             pltpu.VMEM((planes, 2, tok_rows, plane_rows), jnp.bfloat16),
-            pltpu.SemaphoreType.DMA((4,)),
+            pltpu.SemaphoreType.DMA((9,)),
             pltpu.SemaphoreType.DMA((2,)),
             pltpu.SemaphoreType.DMA((expert_total,)),
             pltpu.SemaphoreType.DMA((expert_total,)),
@@ -339,10 +386,8 @@
         stream,
         join_gain[0],
         moe_gain[0],
-        expert_ids[0, 0],
-        gate_scores[0, 0],
-        pack,
-        unpack,
+        expert_ids[0, 0].T,
+        gate_scores[0, 0].T,
         join_weight[0, 0],
         w_gate[0, 0],
         w_up[0, 0],

time: 85.8 us -> 85.6 us (level)
    unnamed x9 -> x11, local copies, waits for them, and re-layouts: 4.79 us -> 4.59 us
where the time goes in v5:
time: 85.6 us; the launch traced here: 85.4 us
  Pallas kernels  80.8 us (94%)
  local copies, waits for them, and re-layouts  4.59 us (5%)
    pallas_call x1, Pallas kernels, body(): pl.pallas_call(functools.partial(kernel, (planes, members, sensor_count,...  80.8 us
    unnamed x11, local copies, waits for them, and re-layouts  4.59 us

profile of v5, /device:TPU:11, one launch (start us, length us, event | category | flops | bytes accessed | tf_op | source)
XLA Modules:
  0.0 85.4 jit_solution(13566148284982154819)
XLA Ops:
  0.0 0.0 copy-start
  0.0 1.0 %copy-done = bf16[1,128,2048]{2,1,0:T(8,128)(2,1)S(1)} copy-done((bf16[1,128,2048]{2,1,0:T(8,128)(2,1)S(1)}, bf16[1,128,2048]{2,1,0:T(8,128)(2,1)}, u32[]{:S(2)}) %copy-start) | copy-done | bytes 524312
  1.0 0.0 copy-start.1
  1.0 0.7 copy-done.1
  1.7 0.0 copy-start.2
  1.7 0.7 copy-done.2
  2.4 0.0 copy-start.3
  2.4 0.7 copy-done.3
  3.1 0.0 copy-start.4
  3.1 0.7 copy-done.4
  3.8 80.8 %shard_map.91 = bf16[128,2048]{1,0:T(8,128)(2,1)S(1)} custom-call(bf16[128,2048]{1,0:T(8,128)(2,1)S(1)} %bitcast.15, bf16[1,2048]{1,0:T(2,128)(2,1)S(1)} %bitcast.16, bf16[1,2048]{1,0:T(2,128)(2,1)S(1)} %bitcast.17, s32[2,128]{1,0:T(2,128)S(1)} %bitcast.18, f32[2,128]{1,0:T(2,128)S(1)} %bitcast.19, bf16[2048,2048]{1,0:T(8,128)(2,1)} %bitcast.20, ...), custom_call_target="tpu_custom_call" | custom-call | tf_op jit(solution)/shard_map/pallas_call | solution.py:344
  84.6 0.8 copy.11
Async XLA Ops:
  0.0 1.0 %copy-start = (bf16[1,128,2048]{2,1,0:T(8,128)(2,1)S(1)}, bf16[1,128,2048]{2,1,0:T(8,128)(2,1)}, u32[]{:S(2)}) copy-start(bf16[1,128,2048]{2,1,0:T(8,128)(2,1)} %param.9) | copy-start | bytes 1572868
  1.0 0.7 copy-start.1
  1.7 0.7 copy-start.2
  2.4 0.7 copy-start.3
  3.1 0.7 copy-start.4
